TPU v7x, 256 devices: a whole 4x4x8 slice. The times are simulated.
256 devices in a mesh: wide: 64 (over z, x, core), rep: 4 (over y).
Axes of the slice: x: 4, y: 4, z: 8, core: 2. Of those that a mesh axis runs over, the one named last changes fastest.
Arguments:
- factor: float32 [32, 1024, 4096], P(None, 'wide'), may hold values from -0.09375 to 0.09375
- inverses: float32 [4, 1, 1024, 1024], P(None, None, 'wide'), as said below
- right_side: float32 [32, 1024, 512], P(None, 'wide', 'rep'), may hold values from -6 to 6
- obs_cells: int32 [4096], replicated, may hold values from 0 to 8388607
- noise: float32 [1024, 4, 8, 1024], P('wide', None, 'rep'), may hold values from -6 to 6
- spectrum: float32 [1024, 8, 1024], P(None, 'rep', 'wide'), may hold values from 0.25 to 4, as said below
Outputs:
- solved: float32 [32, 1024, 512], P(None, 'wide', 'rep')
- correction: float32 [1024, 4, 8, 1024], P('wide', None, 'rep')
Inputs may be any that keep to these rules, and one draw needn't show every extreme that they name: `inverses`: each D_k is lower triangular. spectrum[x, y, z] equals spectrum[(1024 - x) % 1024, y, (1024 - z) % 1024].
All inputs are finite; a program needn't handle non-finite values.
Results may differ from a plain program's by a relative error of at most 0.0001.
Values sent between devices are 32-bit elements; how exact they have to be, the bound alone decides.
No kernel may reach another device: no remote copies, remote signals or barrier semaphores. Data moves between devices by JAX's collectives and lax.ppermute only.
A program may use at most 192 MiB of HBM per device.

v0:
```python
import math

import jax
import jax.numpy as jnp
from jax import lax
from jax.sharding import PartitionSpec as P

PRECISE = lax.Precision.HIGHEST


def subtract_panel(block_rows, factor_rows, unknowns):
    update = jnp.einsum(
        "btc,cs->bts", factor_rows, unknowns, precision=PRECISE, preferred_element_type=jnp.float32
    )
    return block_rows - update


def dft_tables(length):
    counter = jnp.arange(length, dtype=jnp.int32)
    turns = counter[:, None] * counter[None, :] % length
    angle = turns.astype(jnp.float32) * (2.0 * math.pi / length)
    return (jnp.cos(angle), jnp.sin(angle))


def matmul(left, right):
    return jnp.dot(left, right, precision=PRECISE, preferred_element_type=jnp.float32)


def filter_pencil(pencil, spectrum):
    full_x, group_count, y_planes, z_share = pencil.shape[1:]
    cos_x, sin_x = dft_tables(full_x)
    real_in = pencil[0].reshape(full_x, -1)
    imag_in = pencil[1].reshape(full_x, -1)
    real_freq = matmul(cos_x, real_in) + matmul(sin_x, imag_in)
    imag_freq = matmul(cos_x, imag_in) - matmul(sin_x, real_in)
    scale = jnp.broadcast_to(spectrum[:, None], (full_x, group_count, y_planes, z_share)).reshape(
        full_x, -1
    )
    real_freq = real_freq * scale
    imag_freq = imag_freq * scale
    real_back = (matmul(cos_x, real_freq) - matmul(sin_x, imag_freq)) / full_x
    imag_back = (matmul(cos_x, imag_freq) + matmul(sin_x, real_freq)) / full_x
    return jnp.stack([real_back, imag_back]).reshape(2, full_x, group_count, y_planes, z_share)


def per_device(factor, inverses, right_side, obs_cells, noise, spectrum):
    panel_count, panel_blocks, block_rows, panel_width = inverses.shape
    sample_cols = right_side.shape[2]
    wide_index = lax.axis_index("wide")
    work = right_side
    panels = []
    for panel_index in range(panel_count):
        first_blk = panel_index * panel_blocks
        after_blk = first_blk + panel_blocks
        residual = work[first_blk:after_blk]
        local_inverse = inverses[panel_index].reshape(
            panel_blocks * block_rows, panel_blocks, panel_width // panel_blocks
        )

        def fold_rows(total, piece, start, local_inverse=local_inverse):
            return jnp.einsum(
                "rbj,bjs->rs",
                local_inverse,
                piece,
                precision=PRECISE,
                preferred_element_type=jnp.float32,
            )

        start_total = jnp.zeros((panel_blocks * block_rows, sample_cols), jnp.float32)
        own_rows = fold_rows(
            start_total, lax.all_gather(residual, "wide", axis=1, tiled=True), jnp.int32(0)
        )
        own_rows = own_rows.reshape(panel_blocks, block_rows, sample_cols)
        unknowns = lax.all_gather(own_rows, "wide", axis=1, tiled=True).reshape(
            panel_width, sample_cols
        )
        col_start = panel_index * panel_width
        col_end = col_start + panel_width
        below_rows = subtract_panel(
            work[after_blk:], factor[after_blk:, :, col_start:col_end], unknowns
        )
        work = jnp.concatenate([work[:first_blk], own_rows, below_rows], axis=0)
        panels.append(unknowns)
    stacked = jnp.concatenate(panels, axis=0)
    weights = lax.all_gather(stacked[:, 0:1], "rep", axis=1, tiled=True)
    x_cells, field_count, y_planes, z_cells = noise.shape
    all_planes = y_planes * lax.axis_size("rep")
    rep_index = lax.axis_index("rep")
    x_local = obs_cells // (all_planes * z_cells) - wide_index * x_cells
    y_local = obs_cells // z_cells % all_planes - rep_index * y_planes
    z_local = obs_cells % z_cells
    inside = (x_local >= 0) & (x_local < x_cells) & (y_local >= 0) & (y_local < y_planes)
    x_local = jnp.where(inside, x_local, x_cells)
    y_local = jnp.where(inside, y_local, 0)
    field = noise.at[x_local, :, y_local, z_local].add(weights, mode="drop")
    cos_z, sin_z = dft_tables(z_cells)
    flat_rows = field.reshape(x_cells * field_count * y_planes, z_cells)
    real_z = matmul(flat_rows, cos_z)
    imag_z = -matmul(flat_rows, sin_z)
    slab = jnp.stack([real_z, imag_z]).reshape(2, x_cells, field_count, y_planes, z_cells)
    pencil = lax.all_to_all(slab, "wide", split_axis=4, concat_axis=1, tiled=True)
    pencil_back = filter_pencil(pencil, spectrum)
    slab_back = lax.all_to_all(pencil_back, "wide", split_axis=1, concat_axis=4, tiled=True)
    real_rows = slab_back[0].reshape(-1, z_cells)
    imag_rows = slab_back[1].reshape(-1, z_cells)
    filtered = (matmul(real_rows, cos_z) - matmul(imag_rows, sin_z)) / z_cells
    correction = filtered.reshape(x_cells, field_count, y_planes, z_cells)
    return (work, correction)


def solution(mesh):
    return jax.shard_map(
        per_device,
        mesh=mesh,
        in_specs=(
            P(None, "wide", None),
            P(None, None, "wide", None),
            P(None, "wide", "rep"),
            P(),
            P("wide", None, "rep", None),
            P(None, "rep", "wide"),
        ),
        out_specs=(P(None, "wide", "rep"), P("wide", None, "rep", None)),
        check_vma=False,
    )
```

profile of v0, /device:TPU:1, one launch (start us, length us, event | category | flops | bytes accessed | tf_op | source)
XLA Modules:
  0.0 955.8 jit_solution(17367407698595390041)
XLA Ops:
  6.0 54.7 %all_gather.27 = f32[1,1024,128]{2,1,0:T(8,128)S(1)} all-gather(f32[1,16,128]{2,1,0:T(8,128)S(1)} %slice-done), channel_id=1, replica_groups=mesh['wide'=64,'rep'=4] {'wide'}, dimensions={1}, use_global_device_ids=true | all-gather | bytes 532480 | tf_op jit(solution)/shard_map/all_gather | solution.py:71
  61.1 49.2 %all-gather = f32[1024,128]{1,0:T(8,128)S(1)} all-gather(f32[16,128]{1,0:T(8,128)S(1)} %fusion.106), channel_id=2, replica_groups=mesh['wide'=64,'rep'=4] {'wide'}, dimensions={0}, use_global_device_ids=true | all-gather | bytes 532480 | tf_op jit(solution)/shard_map/all_gather | solution.py:74
  113.0 48.0 %all_gather.29 = f32[1,1024,128]{2,0,1:T(1,128)S(1)} all-gather(f32[1,16,128]{2,0,1:T(1,128)S(1)} %slice.88), channel_id=1, replica_groups=mesh['wide'=64,'rep'=4] {'wide'}, dimensions={1}, use_global_device_ids=true | all-gather | bytes 532480 | tf_op jit(solution)/shard_map/all_gather | solution.py:71
  161.3 49.4 %all-gather.1 = f32[1024,128]{1,0:T(8,128)S(1)} all-gather(f32[16,128]{1,0:T(8,128)S(1)} %bitcast.150), channel_id=3, replica_groups=mesh['wide'=64,'rep'=4] {'wide'}, dimensions={0}, use_global_device_ids=true | all-gather | bytes 532480 | tf_op jit(solution)/shard_map/all_gather | solution.py:74
  213.4 48.0 %all_gather.31 = f32[1,1024,128]{2,0,1:T(1,128)S(1)} all-gather(f32[1,16,128]{2,0,1:T(1,128)S(1)} %slice.90), channel_id=1, replica_groups=mesh['wide'=64,'rep'=4] {'wide'}, dimensions={1}, use_global_device_ids=true | all-gather | bytes 532480 | tf_op jit(solution)/shard_map/all_gather | solution.py:71
  261.8 49.6 %all-gather.2 = f32[1024,128]{1,0:T(8,128)S(1)} all-gather(f32[16,128]{1,0:T(8,128)S(1)} %bitcast.152), channel_id=4, replica_groups=mesh['wide'=64,'rep'=4] {'wide'}, dimensions={0}, use_global_device_ids=true | all-gather | bytes 532480 | tf_op jit(solution)/shard_map/all_gather | solution.py:74
  314.0 48.0 %all_gather.33 = f32[1,1024,128]{2,0,1:T(1,128)S(1)} all-gather(f32[1,16,128]{2,0,1:T(1,128)S(1)} %slice.92), channel_id=1, replica_groups=mesh['wide'=64,'rep'=4] {'wide'}, dimensions={1}, use_global_device_ids=true | all-gather | bytes 532480 | tf_op jit(solution)/shard_map/all_gather | solution.py:71
  362.3 49.2 %all-gather.3 = f32[1024,128]{1,0:T(8,128)S(1)} all-gather(f32[16,128]{1,0:T(8,128)S(1)} %bitcast.154), channel_id=5, replica_groups=mesh['wide'=64,'rep'=4] {'wide'}, dimensions={0}, use_global_device_ids=true | all-gather | bytes 532480 | tf_op jit(solution)/shard_map/all_gather | solution.py:74
  431.8 31.6 %scatter_fusion = f32[32768,4]{1,0:T(8,128)} fusion(f32[32768,4]{1,0:T(8,128)} %bitcast.124, s32[4096]{0:T(1024)S(1)} %broadcast_select_fusion, f32[4096,4]{1,0:T(8,128)S(1)} %copy.101), kind=kCustom, calls=%fused_computation | custom fusion | flops 16384 | bytes 212992
  483.7 18.3 %fusion.75 = f32[128,1024]{1,0:T(8,128)S(1)} fusion(f32[128,1024]{1,0:T(8,128)S(1)} %reshape.105), kind=kOutput, calls=%fused_computation.48 | convolution fusion | flops 1625423872 | bytes 1048576 | tf_op jit(solution)/shard_map/dot_general | solution.py:26
  502.7 18.4 %fusion.42 = f32[1,16,4,2,1024]{4,1,3,2,0:T(8,128)S(1)} fusion(f32[16,4,2,1024]{3,2,0,1:T(2,128)S(1)} %bitcast.139), kind=kOutput, calls=%fused_computation.37 | convolution fusion | flops 1625292800 | bytes 1048576 | tf_op jit(solution)/shard_map/dot_general | solution.py:26
  552.9 27.7 %all-to-all-done = f32[64,1,4096]{2,1,0:T(1,128)S(1)} async-done(((f32[64,1,4096]{2,1,0:T(1,128)}), f32[64,1,4096]{2,1,0:T(1,128)S(1)}, u32[]{:S(2)}, u32[]{:S(2)}) %all-to-all-start) | async-done | bytes 1048608 | tf_op jit(solution)/shard_map/all_to_all | solution.py:101
  597.0 14.7 %copy.121 = f32[2,16,4,2,64,16]{5,4,1,3,2,0:T(8,128)} copy(f32[2,16,4,2,64,16]{1,3,2,0,5,4:T(2,128)} %bitcast.131) | data formatting | bytes 2097152 | tf_op jit(solution)/shard_map/all_to_all | solution.py:101
  630.5 18.7 %fusion.23 = f32[1024,128]{1,0:T(8,128)S(1)} fusion(f32[1024,128]{0,1:T(8,128)S(1)} %reshape_squeeze.17), kind=kOutput, calls=%fused_computation.28 | convolution fusion | flops 1625292800 | bytes 1048576 | tf_op jit(solution)/shard_map/dot_general | solution.py:26
  659.9 18.6 %fusion.27 = f32[1024,128]{1,0:T(8,128)S(1)} fusion(f32[1024,128]{0,1:T(8,128)S(1)} %reshape_squeeze.16), kind=kOutput, calls=%fused_computation.30 | convolution fusion | flops 1625292800 | bytes 1048576 | tf_op jit(solution)/shard_map/dot_general | solution.py:26
  678.5 19.2 %fusion.69 = f32[1024,128]{1,0:T(8,128)S(1)} fusion(f32[1024,128]{1,0:T(8,128)S(1)} %copy.110, f32[1024,128]{1,0:T(8,128)S(1)} %fusion.23, f32[1024,128]{0,1:T(8,128)S(1)} %reshape_squeeze.16), kind=kOutput, calls=%fused_computation.46 | convolution fusion | flops 1625554944 | bytes 2097152 | tf_op jit(solution)/shard_map/dot_general | solution.py:26
  697.7 20.3 %fusion.21 = f32[1024,128]{0,1:T(8,128)S(1)} fusion(f32[1024,128]{1,0:T(8,128)S(1)} %fusion.69), kind=kOutput, calls=%fused_computation.27 | convolution fusion | flops 1625292800 | bytes 1048576 | tf_op jit(solution)/shard_map/dot_general | solution.py:26
  718.0 18.8 %fusion.72 = f32[1024,128]{1,0:T(8,128)S(1)} fusion(f32[1024,128]{1,0:T(8,128)S(1)} %copy.110, f32[1024,128]{1,0:T(8,128)S(1)} %fusion.27, f32[1024,128]{0,1:T(8,128)S(1)} %reshape_squeeze.17), kind=kOutput, calls=%fused_computation.47 | convolution fusion | flops 1625554944 | bytes 2097152 | tf_op jit(solution)/shard_map/dot_general | solution.py:26
  736.8 20.5 %fusion.25 = f32[1024,128]{0,1:T(8,128)S(1)} fusion(f32[1024,128]{1,0:T(8,128)S(1)} %fusion.72), kind=kOutput, calls=%fused_computation.29 | convolution fusion | flops 1625292800 | bytes 1048576 | tf_op jit(solution)/shard_map/dot_general | solution.py:26
  757.4 20.2 %fusion.63 = f32[1024,128]{0,1:T(8,128)S(1)} fusion(f32[1024,128]{0,1:T(8,128)S(1)} %fusion.21, f32[1024,128]{1,0:T(8,128)S(1)} %fusion.72), kind=kOutput, calls=%fused_computation.44 | convolution fusion | flops 1625554944 | bytes 1572864 | tf_op jit(solution)/shard_map/dot_general | solution.py:26
  777.6 20.4 %fusion.66 = f32[1024,128]{0,1:T(8,128)S(1)} fusion(f32[1024,128]{0,1:T(8,128)S(1)} %fusion.25, f32[1024,128]{1,0:T(8,128)S(1)} %fusion.69), kind=kOutput, calls=%fused_computation.45 | convolution fusion | flops 1625554944 | bytes 1572864 | tf_op jit(solution)/shard_map/dot_general | solution.py:26
  832.9 22.4 %all-to-all-done.1 = f32[64,1,4096]{2,1,0:T(1,128)S(1)} async-done(((f32[64,1,4096]{2,1,0:T(1,128)}), f32[64,1,4096]{2,1,0:T(1,128)S(1)}, u32[]{:S(2)}, u32[]{:S(2)}) %all-to-all-start.1) | async-done | bytes 1048608 | tf_op jit(solution)/shard_map/all_to_all | solution.py:103
  905.6 18.5 %fusion.19 = f32[128,1024]{1,0:T(8,128)S(1)} fusion(f32[128,1024]{1,0:T(8,128)S(1)} %reshape_squeeze.18), kind=kOutput, calls=%fused_computation.26 | convolution fusion | flops 1625292800 | bytes 1048576 | tf_op jit(solution)/shard_map/dot_general | solution.py:26
  935.6 18.6 %fusion.60 = f32[128,1024]{1,0:T(8,128)S(1)} fusion(f32[128,1024]{1,0:T(8,128)S(1)} %fusion.19, f32[128,1024]{1,0:T(8,128)S(1)} %reshape_squeeze.19), kind=kOutput, calls=%fused_computation.43 | convolution fusion | flops 1625554944 | bytes 1572864 | tf_op jit(solution)/shard_map/dot_general | solution.py:26
  (75 shorter events, 231.4 us)
Async XLA Ops:
  2.4 3.6 slice-start
  2.4 58.3 %copy-start.1 = (f32[4,1,16,1024]{3,2,1,0:T(8,128)S(1)}, f32[4,1,16,1024]{3,2,1,0:T(8,128)}, u32[]{:S(2)}) copy-start(f32[4,1,16,1024]{3,2,1,0:T(8,128)} %param.7) | copy-start | bytes 786436
  2.5 107.8 %slice-start.1 = ((f32[32,16,128]{2,1,0:T(8,128)}), f32[31,16,128]{2,1,0:T(8,128)S(1)}, s32[]{:S(2)}) async-start(f32[32,16,128]{2,1,0:T(8,128)} %param.8), calls=%async_computation.3 | async-start | bytes 507904 | tf_op jit(solution)/shard_map/slice | solution.py:80
  210.7 200.8 %copy-start = (f32[16,4,2,1024]{3,2,1,0:T(2,128)S(1)}, f32[16,4,2,1024]{3,2,1,0:T(2,128)}, u32[]{:S(2)}) copy-start(f32[16,4,2,1024]{3,2,1,0:T(2,128)} %param.10) | copy-start | bytes 1572868
  411.5 8.7 copy-start.3
  411.5 8.7 copy-start.5
  411.5 8.9 copy-start.4
  529.8 22.8 %copy-start.2 = (f32[1024,2,16]{0,2,1:T(8,128)S(1)}, f32[1024,2,16]{0,2,1:T(8,128)}, u32[]{:S(2)}) copy-start(f32[1024,2,16]{0,2,1:T(8,128)} %param.11) | copy-start | bytes 393220
  544.1 36.6 %all-to-all-start = ((f32[64,1,4096]{2,1,0:T(1,128)}), f32[64,1,4096]{2,1,0:T(1,128)S(1)}, u32[]{:S(2)}, u32[]{:S(2)}) async-start(f32[64,1,4096]{2,1,0:T(1,128)} %reshape.136), calls=%async_computation | async-start | bytes 2097152 | tf_op jit(solution)/shard_map/all_to_all | solution.py:101
  820.6 34.7 %all-to-all-start.1 = ((f32[64,1,4096]{2,1,0:T(1,128)}), f32[64,1,4096]{2,1,0:T(1,128)S(1)}, u32[]{:S(2)}, u32[]{:S(2)}) async-start(f32[64,1,4096]{2,1,0:T(1,128)} %reshape.138), calls=%async_computation.1 | async-start | bytes 2097152 | tf_op jit(solution)/shard_map/all_to_all | solution.py:103
where the time goes:
time: 966 us; the launch traced here: 956 us
  blocking collectives  406 us (42%)
  matrix products  243 us (25%)
  local copies, waits for them, and re-layouts  201 us (21%)
  waiting for transfers between devices  50.2 us (5%)
  other arithmetic  39.2 us (4%)
  starting transfers between devices  15.4 us (2%)
    dot_general x12, matrix products, matmul(): jnp.dot(left, right, precision=PRECISE, preferred_element_type=jnp.float32)  231 us
    all_gather x4, blocking collectives, per_device(): lax.all_gather(residual, 'wide', axis=1, tiled=True)  199 us
    all_gather x4, blocking collectives, per_device(): lax.all_gather(own_rows, 'wide', axis=1, tiled=True)  197 us
    unnamed x21, local copies, waits for them, and re-layouts  73.4 us
    unnamed x4, other arithmetic  31.8 us
    all_to_all x1, waiting for transfers between devices, per_device(): lax.all_to_all(slab, 'wide', split_axis=4, concat_axis=1, tiled=True)  27.7 us
    all_to_all x1, waiting for transfers between devices, per_device(): lax.all_to_all(pencil_back, 'wide', split_axis=1, concat_axis=4, tiled=True)  22.4 us
  transfers between devices with their start and end apart: 2, of which 2 were waited for; matrix products, arithmetic and copies ran while one was open for 1% of the time, Pallas kernels for 0%

commit v1 on v0

v1 whole, which is shorter than its diff:
```python
import functools
import math

import jax
import jax.numpy as jnp
import numpy as np
from jax import lax
from jax.experimental import pallas as pl
from jax.experimental.pallas import tpu as pltpu
from jax.sharding import Mesh, PartitionSpec as P

F32 = jnp.float32
BF16 = jnp.bfloat16
WIDE = ("z", "x", "core")
LENGTH = 1024
COLS = 24
NN = (((1,), (0,)), ((), ()))
NT = (((1,), (1,)), ((), ()))
LIMIT = pltpu.CompilerParams(vmem_limit_bytes=56 * 1024 * 1024)


def halves(table):
    high = table.astype(np.float32).astype(jnp.bfloat16)
    low = (table - high.astype(np.float64)).astype(np.float32).astype(jnp.bfloat16)
    return (np.asarray(high), np.asarray(low))


def z_frequencies(owner, xp):
    step = xp.arange(16) % 8
    part = xp.arange(16) // 8
    freq = 16 * owner + step + xp.where(owner >= 32, 1, 0)
    lone = (owner == 0) & (step == 0) & (part == 1)
    return (xp.where(lone, 512, freq), xp.where(lone, 0, 256 * part))


def z_table():
    rows = []
    cells = np.arange(LENGTH)
    for owner in range(64):
        freq, phase = z_frequencies(np.int64(owner), np)
        turn = (freq[:, None] * cells[None, :] + phase[:, None]) % LENGTH
        rows.append(np.cos(2.0 * np.pi * turn / LENGTH))
    return np.concatenate(rows)


def x_table():
    cells = np.arange(LENGTH)
    freq = np.concatenate([np.arange(512), np.arange(512)])
    phase = np.repeat([0, 256], 512)
    freq[512], phase[512] = 512, 0
    turn = (freq[:, None] * cells[None, :] + phase[:, None]) % LENGTH
    return np.cos(2.0 * np.pi * turn / LENGTH)


def split(value):
    high = value.astype(BF16)
    low = (value - high.astype(F32)).astype(BF16)
    return (high, low)


def dot(left, right, dims):
    return lax.dot_general(left, right, dims, preferred_element_type=F32)


def dot_nt(left, right):
    left_high, left_low = split(left)
    right_high, right_low = split(right)
    rows = left.shape[0]
    both = dot(jnp.concatenate([left_high, left_low]), right_high, NT)
    return both[:rows] + both[rows:] + dot(left_high, right_low, NT)


def table_nn(high, low, value):
    value_high, value_low = split(value)
    cols = value.shape[1]
    both = dot(high, jnp.concatenate([value_high, value_low], axis=1), NN)
    return both[:, :cols] + both[:, cols:] + dot(low, value_high, NN)


def swap_groups(value):
    row = lax.broadcasted_iota(jnp.int32, value.shape, 0)
    lane = lax.broadcasted_iota(jnp.int32, value.shape, 1)
    for bit in range(4):
        step = 1 << bit
        row_bit = (row >> bit) & 1
        lane_bit = (lane >> (3 + bit)) & 1
        up = pltpu.roll(pltpu.roll(value, LENGTH - step, 0), 8 * step, 1)
        down = pltpu.roll(pltpu.roll(value, step, 0), 128 - 8 * step, 1)
        value = jnp.where(row_bit == lane_bit, value, jnp.where(lane_bit == 1, up, down))
    return value


def pack_kernel(inverse_ref, noise_ref, high_ref, low_ref, out_ref):
    lane = lax.broadcasted_iota(jnp.int32, (64, 128), 1) // 16
    for r in range(8):
        total = jnp.zeros((64, 128), F32)
        for z in range(8):
            piece = inverse_ref[:, 128 * z : 128 * z + 128]
            piece = pltpu.roll(piece, (16 * (z - r)) % 128, 1) if z != r else piece
            total = jnp.where(lane == z, piece, total)
        for z in range(8):
            out_ref[8 * z + r, 0:64, :] = total
    noise_high, noise_low = split(noise_ref[...])
    both = dot(high_ref[...], jnp.concatenate([noise_high, noise_low]), NT)
    slots = both[:, :128] + both[:, 128:] + dot(low_ref[...], noise_high, NT)
    out_ref[:, 64:80, :] = slots.reshape(64, 16, 128)


def first_kernel(start_ref, inverse_ref, out_ref):
    out_ref[...] = dot_nt(start_ref[0], inverse_ref[...].reshape(LENGTH, 128))


def step_kernel(panel, *refs):
    parts, rest = refs[:4], refs[4:]
    start_ref, inverse_ref = rest[:2]
    factor_refs = rest[2 : 2 + panel]
    older_refs = rest[2 + panel : 1 + 2 * panel]
    out_ref, unknown_ref = rest[1 + 2 * panel :]
    unknown = (parts[0][...] + parts[1][...]) + (parts[2][...] + parts[3][...])
    unknown_ref[...] = unknown
    work = start_ref[0]
    for ref, factor_ref in zip(older_refs, factor_refs):
        work = work - dot_nt(ref[...], factor_ref[...].reshape(128, LENGTH))
    work = work - dot_nt(unknown, factor_refs[-1][...].reshape(128, LENGTH))
    out_ref[...] = dot_nt(work, inverse_ref[...].reshape(LENGTH, 128))


def spectrum_kernel(index_ref, spectrum_ref, extra_ref, even_ref, odd_ref):
    owner = index_ref[0]
    row = lax.broadcasted_iota(jnp.int32, (32, 128), 0)
    lane = lax.broadcasted_iota(jnp.int32, (32, 128), 1)
    lone = (owner == 0) & (lane // 8 == 8)
    same_y = row // 16 == lane % 2
    same_z = row % 16 == (lane // 8) % 8 + jnp.where(owner >= 32, 1, 0)
    pick = jnp.where(same_y & same_z & jnp.logical_not(lone), 1.0, 0.0).astype(BF16)
    extra_pick = jnp.where(lone & (row == lane % 2), 1.0, 0.0)[:8].astype(BF16)

    def exact(value, choose):
        high = value.astype(BF16)
        rest = value - high.astype(F32)
        middle = rest.astype(BF16)
        low = (rest - middle.astype(F32)).astype(BF16)
        return choose(high) + (choose(middle) + choose(low))

    wanted = exact(spectrum_ref[...], lambda part: dot(part, pick, NN))
    wanted = wanted + exact(
        jnp.transpose(extra_ref[...]), lambda part: dot(part, extra_pick, NN)
    )
    at_row = lax.broadcasted_iota(jnp.int32, (512, 512), 0)
    at_col = lax.broadcasted_iota(jnp.int32, (512, 512), 1)
    mirror = jnp.where(at_row + at_col == 512, 1.0, 0.0).astype(BF16)
    plus = wanted[:512]
    upper = wanted[512:]
    minus = exact(upper, lambda part: dot(mirror, part, NN))
    first = lax.broadcasted_iota(jnp.int32, (512, 128), 0) == 0
    minus = jnp.where(first, plus, minus)
    lanes = lax.broadcasted_iota(jnp.int32, (512, 128), 1)
    alone = (owner == 0) & ((lanes // 8) % 8 == 0)
    scale = jnp.where(first, 1.0, 2.0) * jnp.where(alone, 1.0, 2.0) / (LENGTH * LENGTH)
    even = (plus + minus) * (0.5 * scale)
    even_ref[0:512] = even
    even_ref[512:1024] = jnp.where(first, upper * scale, even)
    odd = (plus - minus) * (0.5 * scale)
    odd_ref[...] = jnp.where(lanes < 64, -odd, odd)


def add_weights(pencil, cell_ref, wave_ref, plane_ref, weights):
    doubled = jnp.concatenate(
        [weights[g : g + 1] * plane_ref[y : y + 1] for g in range(4) for y in range(2)]
    )
    waves = (wave_ref[...][:, None, :] * doubled[None]).reshape(128, LENGTH)
    cells = lax.broadcasted_iota(jnp.int32, (LENGTH, LENGTH), 0)
    chosen = jnp.where(cells == cell_ref[...], 1.0, 0.0).astype(BF16)
    high, low = split(waves)
    both = dot(chosen, jnp.concatenate([high, low]), NT)
    return pencil + both[:, :128] + both[:, 128:]


def open_kernel(slab_ref, cell_ref, wave_ref, plane_ref, unknown_ref, out_ref):
    pencil = swap_groups(slab_ref[...].reshape(LENGTH, 128))
    out_ref[...] = add_weights(pencil, cell_ref, wave_ref, plane_ref, unknown_ref[16:20])


def add_kernel(pencil_ref, cell_ref, wave_ref, plane_ref, unknown_ref, out_ref):
    out_ref[...] = add_weights(
        pencil_ref[...], cell_ref, wave_ref, plane_ref, unknown_ref[16:20]
    )


def filter_kernel(
    pencil_ref, cell_ref, wave_ref, plane_ref, a_ref, b_ref, c_ref, d_ref,
    high_ref, low_ref, back_high_ref, back_low_ref, even_ref, odd_ref, out_ref,
):
    weights = (a_ref[16:20] + b_ref[16:20]) + (c_ref[16:20] + d_ref[16:20])
    pencil = add_weights(pencil_ref[...], cell_ref, wave_ref, plane_ref, weights)
    freq = table_nn(high_ref[...], low_ref[...], pencil)
    real, imag = freq[:512], freq[512:]
    odd = odd_ref[...]
    real_out = even_ref[0:512] * real + odd * pltpu.roll(imag, 64, 1)
    imag_out = even_ref[512:1024] * imag - odd * pltpu.roll(real, 64, 1)
    back = table_nn(
        back_high_ref[...], back_low_ref[...], jnp.concatenate([real_out, imag_out])
    )
    out_ref[...] = swap_groups(back).reshape(64, 16, 128)


def close_kernel(slots_ref, high_ref, low_ref, out_ref):
    rows = jnp.transpose(slots_ref[...].reshape(LENGTH, 128))
    rows_high, rows_low = split(rows)
    both = dot(jnp.concatenate([rows_high, rows_low]), high_ref[...], NN)
    out_ref[...] = both[:128] + both[128:] + dot(rows_high, low_ref[...], NN)


def update_kernel(first_panel, index_ref, base_ref, factor_ref, unknown_ref, out_ref):
    block = pl.program_id(0)
    own = index_ref[0] * 16
    row = lax.broadcasted_iota(jnp.int32, (128, LENGTH), 0) + block * 128
    col = lax.broadcasted_iota(jnp.int32, (128, LENGTH), 1)
    base = base_ref[...].reshape(128, 128)
    if first_panel == 0:
        base_row = lax.broadcasted_iota(jnp.int32, (128, 128), 0) + block * 128
        base = jnp.where(base_row < 64, 0.0, base)
    for step in range(2):
        panel = first_panel + step
        rows = factor_ref[:, :, LENGTH * step : LENGTH * (step + 1)].reshape(128, LENGTH)
        mine = (row // 16 == panel) & (col == own + row % 16)
        rows = jnp.where(row < 64, jnp.where(mine, -1.0, 0.0), rows)
        unknown = unknown_ref[:, 16 * step : 16 * step + 16, :].reshape(128, LENGTH)
        base = base - dot_nt(rows, unknown)
    out_ref[...] = base.reshape(8, 16, 128)


def spec(*shape):
    return pl.BlockSpec(shape, lambda *_: (0,) * len(shape))


def block_at(shape, place):
    return pl.BlockSpec(shape, lambda *_: place)


def cost(flops, moved):
    return pl.CostEstimate(flops=flops, bytes_accessed=moved, transcendentals=0)


def shape_of(*shape):
    return jax.ShapeDtypeStruct(shape, F32)


def call(body, name, in_specs, out_specs, out_shape, flops, moved):
    return pl.pallas_call(
        body,
        grid=(1,),
        in_specs=in_specs,
        out_specs=out_specs,
        out_shape=out_shape,
        compiler_params=LIMIT,
        cost_estimate=cost(flops, moved),
        name=name,
    )


def ring(size, step):
    return [(place, (place + step) % size) for place in range(size)]


def share(partial):
    total = partial + lax.ppermute(partial, "core", ring(2, 1))
    return [total] + [lax.ppermute(total, "x", ring(4, step)) for step in (1, 2, 3)]


def update(first_panel, index, base, factor, unknowns):
    return pl.pallas_call(
        functools.partial(update_kernel, first_panel),
        grid=(4,),
        in_specs=[
            pl.BlockSpec(memory_space=pltpu.SMEM),
            pl.BlockSpec((8, 16, 128), lambda i: (i, 0, 0)),
            pl.BlockSpec((8, 16, 2 * LENGTH), lambda i: (i, 0, first_panel // 2)),
            spec(8, 32, LENGTH),
        ],
        out_specs=pl.BlockSpec((8, 16, 128), lambda i: (i, 0, 0)),
        out_shape=shape_of(32, 16, 128),
        compiler_params=LIMIT,
        cost_estimate=cost(3 * 2 * 512 * 2048 * 128, 5_500_000),
        name="update",
    )(index, base, factor, unknowns)


def per_device(factor, inverses, right_side, obs_cells, noise, spectrum):
    z_high, z_low = (jnp.asarray(t) for t in halves(z_table()))
    x_high, x_low = (jnp.asarray(t) for t in halves(x_table()))
    back_high, back_low = (jnp.asarray(t) for t in halves(x_table().T))
    wide = lax.axis_index(WIDE).astype(jnp.int32)
    index = wide.reshape(1)

    lower = jnp.concatenate(
        [
            factor[k, :, LENGTH * j : LENGTH * (j + 1)]
            for k in range(1, 4)
            for j in range(k)
        ]
    )
    lower = lax.all_gather(lower, "z")

    packed = call(
        pack_kernel,
        "pack",
        [spec(64, LENGTH), spec(128, LENGTH)] + [spec(LENGTH, LENGTH)] * 2,
        spec(64, 80, 128),
        shape_of(64, 80, 128),
        3 * 2 * 128 * LENGTH * LENGTH,
        8_000_000,
    )(inverses.reshape(64, LENGTH), noise.reshape(128, LENGTH), z_high, z_low)
    packed = lax.all_to_all(packed, WIDE, 0, 0)

    sides = right_side[:4].reshape(64, 128).T
    weight_side = lax.all_to_all(
        jnp.broadcast_to(sides[None, 0:1], (4, 1, 64)), "y", 0, 0
    ).reshape(4, 64)
    sides = jnp.concatenate(
        [
            sides.reshape(8, 16, 64),
            jnp.broadcast_to(weight_side[None], (8, 4, 64)),
            jnp.zeros((8, 4, 64), F32),
        ],
        axis=1,
    )
    sides = lax.all_to_all(sides, "z", 0, 0)
    sides = sides.reshape(8, COLS, 4, 16).transpose(2, 1, 0, 3).reshape(4, COLS, 128)

    cell_x = (obs_cells // (8 * LENGTH)).reshape(1, 4096)
    plane = obs_cells // LENGTH % 8 - 2 * lax.axis_index("y")
    planes = jnp.stack([plane == 0, plane == 1]).astype(F32)
    freq, phase = z_frequencies(wide, jnp)
    turn = (freq[:, None] * (obs_cells % LENGTH)[None, :] + phase[:, None]) % LENGTH
    waves = jnp.cos(turn.astype(F32) * (2.0 * math.pi / LENGTH))

    extra = lax.ppermute(spectrum[:, :, 0].T, WIDE, [(32, 0)])
    extra = jnp.concatenate([extra, jnp.zeros((6, LENGTH), F32)])
    even, odd = call(
        spectrum_kernel,
        "spectrum",
        [pl.BlockSpec(memory_space=pltpu.SMEM), spec(LENGTH, 32), spec(8, LENGTH)],
        [spec(LENGTH, 128), spec(512, 128)],
        [shape_of(LENGTH, 128), shape_of(512, 128)],
        300_000_000,
        1_500_000,
    )(index, spectrum.reshape(LENGTH, 32), extra)

    obs_specs = lambda k: [
        block_at((1, LENGTH), (0, k)),
        block_at((16, LENGTH), (0, k)),
        block_at((2, LENGTH), (0, k)),
    ]

    partial = call(
        first_kernel,
        "first",
        [spec(1, COLS, 128), spec(64, 16, 128)],
        spec(COLS, LENGTH),
        shape_of(COLS, LENGTH),
        20_000_000,
        700_000,
    )(sides, packed)
    parts = share(partial)
    unknowns = []
    halves_done = []
    pencil = None
    for panel in range(1, 4):
        first_block = panel * (panel - 1) // 2
        partial, unknown = call(
            functools.partial(step_kernel, panel),
            f"step{panel}",
            [spec(COLS, LENGTH)] * 4
            + [
                block_at((1, COLS, 128), (panel, 0, 0)),
                block_at((64, 16, 128), (0, panel, 0)),
            ]
            + [block_at((8, 16, LENGTH), (0, first_block + j, 0)) for j in range(panel)]
            + [spec(COLS, LENGTH)] * (panel - 1),
            [spec(COLS, LENGTH)] * 2,
            [shape_of(COLS, LENGTH)] * 2,
            40_000_000,
            1_500_000,
        )(*parts, sides, packed, *([lower] * panel), *unknowns)
        unknowns.append(unknown)
        parts = share(partial)
        body = open_kernel if panel == 1 else add_kernel
        start = packed if panel == 1 else pencil
        start_spec = block_at((64, 16, 128), (0, 4, 0)) if panel == 1 else spec(LENGTH, 128)
        pencil = call(
            body,
            f"pencil{panel}",
            [start_spec] + obs_specs(panel - 1) + [spec(COLS, LENGTH)],
            spec(LENGTH, 128),
            shape_of(LENGTH, 128),
            2 * 2 * 128 * LENGTH * LENGTH,
            1_500_000,
        )(start, cell_x, waves, planes, unknown)
        if panel == 2:
            gathered = lax.all_gather(
                jnp.concatenate([unknowns[0][:16], unknowns[1][:16]]), "z"
            )
            halves_done = update(0, index, right_side, factor, gathered)

    slots = call(
        filter_kernel,
        "filter",
        [spec(LENGTH, 128)]
        + obs_specs(3)
        + [spec(COLS, LENGTH)] * 4
        + [spec(LENGTH, LENGTH)] * 4
        + [spec(LENGTH, 128), spec(512, 128)],
        spec(64, 16, 128),
        shape_of(64, 16, 128),
        8 * 2 * 128 * LENGTH * LENGTH,
        11_000_000,
    )(pencil, cell_x, waves, planes, *parts, x_high, x_low, back_high, back_low, even, odd)
    slots = lax.all_to_all(slots, WIDE, 0, 0)

    last = (parts[0] + parts[1]) + (parts[2] + parts[3])
    gathered = lax.all_gather(jnp.concatenate([unknowns[2][:16], last[:16]]), "z")
    solved = update(2, index, halves_done, factor, gathered)

    correction = call(
        close_kernel,
        "close",
        [spec(64, 16, 128)] + [spec(LENGTH, LENGTH)] * 2,
        spec(128, LENGTH),
        shape_of(128, LENGTH),
        3 * 2 * 128 * LENGTH * LENGTH,
        5_500_000,
    )(slots, z_high, z_low)
    return (solved, correction.reshape(16, 4, 2, LENGTH))


def solution(mesh):
    grid = Mesh(mesh.devices.reshape(8, 4, 2, 4), ("z", "x", "core", "y"))
    return jax.shard_map(
        per_device,
        mesh=grid,
        in_specs=(
            P(None, WIDE, None),
            P(None, None, WIDE, None),
            P(None, WIDE, "y"),
            P(),
            P(WIDE, None, "y", None),
            P(None, "y", WIDE),
        ),
        out_specs=(P(None, WIDE, "y"), P(WIDE, None, "y", None)),
        check_vma=False,
    )
```

time: 966 us -> 269 us (0.28)
  blocking collectives: 406 us -> 28 us
  matrix products: 243 us -> 0 us
  local copies, waits for them, and re-layouts: 201 us -> 22.9 us
  Pallas kernels: 0 us -> 53.3 us
  waiting for transfers between devices: 50.2 us -> 94.9 us
  other arithmetic: 39.2 us -> 8.82 us
  starting transfers between devices: 15.4 us -> 45.6 us
  between operations: 1.57 us -> 14 us
    all_gather x9 -> x0, blocking collectives: 406 us -> none  [the longest x4 199 us: per_device(): lax.all_gather(residual, 'wide', axis=1, tiled=True)]
    dot_general x20 -> x0, matrix products: 243 us -> none  [the longest x12 231 us: matmul(): jnp.dot(left, right, precision=PRECISE, preferred_element_type=jnp.float32)]
    unnamed x21 -> x48, local copies, waits for them, and re-layouts: 73.4 us -> 10.3 us
    pallas_call x0 -> x13, Pallas kernels: none -> 53.3 us  [the longest x2 11.1 us: update(): pl.pallas_call(functools.partial(update_kernel, first_panel), grid=(4,),...]
    slice x17 -> x6, local copies, waits for them, and re-layouts: 48.5 us -> 3.41 us  [the longest x1 0.85 us: per_device(): unknowns[0][:16]]
    another operation x8 -> x2, local copies, waits for them, and re-layouts: 37.3 us -> 0.04 us  [per_device(): planes = jnp.stack([plane == 0, plane == 1]).astype(F32)]
    unnamed x4 -> x0, other arithmetic: 31.8 us -> none
    all_to_all x3 -> x2, local copies, waits for them, and re-layouts: 29.9 us -> 0.64 us  [per_device(): sides = lax.all_to_all(sides, 'z', 0, 0)]
  transfers between devices with their start and end apart: 2 -> 23, of which waited for: 2 -> 13; matrix products, arithmetic and copies ran while one was open for 1% -> 9% of each run, Pallas kernels for 0% -> 17%
where the time goes in v1:
time: 269 us; the launch traced here: 268 us
  waiting for transfers between devices  94.9 us (35%)
  Pallas kernels  53.3 us (20%)
  starting transfers between devices  45.6 us (17%)
  blocking collectives  28 us (10%)
  local copies, waits for them, and re-layouts  22.9 us (9%)
  between operations  14 us (5%)
  other arithmetic  8.82 us (3%)
    all_to_all x1, waiting for transfers between devices, per_device(): packed = lax.all_to_all(packed, WIDE, 0, 0)  76.1 us
    all_to_all x1, blocking collectives, per_device(): slots = lax.all_to_all(slots, WIDE, 0, 0)  28 us
    ppermute x12, starting transfers between devices, share(): lax.ppermute(total, 'x', ring(4, step))  16.1 us
    ppermute x12, waiting for transfers between devices, share(): lax.ppermute(total, 'x', ring(4, step))  14.2 us
    all_to_all x1, starting transfers between devices, per_device(): packed = lax.all_to_all(packed, WIDE, 0, 0)  11.5 us
    pallas_call x2, Pallas kernels, update(): pl.pallas_call(functools.partial(update_kernel, first_panel), grid=(4,),...  11.1 us
    unnamed x48, local copies, waits for them, and re-layouts  10.3 us
    pallas_call x1, Pallas kernels, per_device(): call(filter_kernel, 'filter', [spec(LENGTH, 128)] + obs_specs(3) + [spec(...  9.55 us
  transfers between devices with their start and end apart: 23, of which 13 were waited for; matrix products, arithmetic and copies ran while one was open for 9% of the time, Pallas kernels for 17%

profile of v1, /device:TPU:1, one launch (start us, length us, event | category | flops | bytes accessed | tf_op | source)
XLA Modules:
  0.0 267.6 jit_solution(8432126674454019946)
XLA Ops:
  8.6 5.0 %all-to-all-start = ((f32[4,1,64]{2,1,0:T(1,128)}), f32[4,1,64]{2,1,0:T(1,128)S(1)}, u32[]{:S(2)}, u32[]{:S(2)}) async-start(f32[4,1,64]{2,1,0:T(1,128)} %broadcast_in_dim.28), calls=%async_computation | async-start | bytes 4096 | tf_op jit(solution)/shard_map/all_to_all | solution.py:317
  20.5 8.2 %all-to-all-start.1 = ((f32[8,1,1536]{2,1,0:T(1,128)}), f32[8,1,1536]{2,1,0:T(1,128)S(1)}, u32[]{:S(2)}, u32[]{:S(2)}) async-start(f32[8,1,1536]{2,1,0:T(1,128)} %reshape.88), calls=%async_computation.1 | async-start | bytes 98304 | tf_op jit(solution)/shard_map/all_to_all | solution.py:328
  28.7 2.2 reshape.80.noise_ref
  30.9 5.3 %pack.1 = f32[64,80,128]{2,1,0:T(8,128)} custom-call(f32[64,1024]{1,0:T(8,128)} %bitcast.46, f32[128,1024]{1,0:T(8,128)} %reshape.80.noise_ref, bf16[1024,1024]{1,0:T(8,128)(2,1)} %constant.132.clone.high_ref, bf16[1024,1024]{1,0:T(8,128)(2,1)} %constant.133.clone.low_ref), custom_call_target="tpu_custom_call" | custom-call | flops 805306368 | bytes 8000000 | tf_op jit(solution)/shard_map/pack/pallas_call | solution.py:305
  36.2 11.5 %all-to-all-start.2 = ((f32[64,80,128]{2,1,0:T(8,128)}), f32[64,80,128]{2,1,0:T(8,128)S(1)}, u32[]{:S(2)}, u32[]{:S(2)}) async-start(f32[64,80,128]{2,1,0:T(8,128)} %pack.1), calls=%async_computation.2 | async-start | bytes 5242880 | tf_op jit(solution)/shard_map/all_to_all | solution.py:314
  50.2 76.1 %all-to-all-done.2.inverse_ref.refs_5_.slab_ref = f32[64,80,128]{2,1,0:T(8,128)S(1)} async-done(((f32[64,80,128]{2,1,0:T(8,128)}), f32[64,80,128]{2,1,0:T(8,128)S(1)}, u32[]{:S(2)}, u32[]{:S(2)}) %all-to-all-start.2) | async-done | bytes 2621472 | tf_op jit(solution)/shard_map/all_to_all | solution.py:314
  133.7 2.4 collective-permute-start.2
  137.8 3.0 %collective-permute-done.2.refs_2_ = f32[24,1024]{1,0:T(8,128)S(1)} collective-permute-done((f32[24,1024]{1,0:T(8,128)S(1)}, f32[24,1024]{1,0:T(8,128)S(1)}, u32[]{:S(2)}, u32[]{:S(2)}) %collective-permute-start.2) | collective-permute-done | bytes 98336 | tf_op jit(solution)/shard_map/ppermute | solution.py:268
  141.4 2.6 step1.1
  148.5 2.2 collective-permute-start.6
  156.6 2.9 %step2.1 = (f32[24,1024]{1,0:T(8,128)}, f32[24,1024]{1,0:T(8,128)}) custom-call(f32[24,1024]{1,0:T(8,128)} %copy-done.4, f32[24,1024]{1,0:T(8,128)} %copy-done.12, f32[24,1024]{1,0:T(8,128)} %copy-done.14, f32[24,1024]{1,0:T(8,128)} %copy-done.15, f32[4,24,128]{2,1,0:T(8,128)} %reshape.78.start_ref.refs_4_, f32[64,80,128]{2,1,0:T(8,128)} %copy-done, ...), custom_call_target="tpu_custom_call" | custom-call | flops 40000000 | bytes 1500000 | tf_op jit(solution)/shard_map/step2/pallas_call | solution.py:371
  165.9 2.2 collective-permute-start.10
  174.0 3.3 %step3.1 = (f32[24,1024]{1,0:T(8,128)}, f32[24,1024]{1,0:T(8,128)}) custom-call(f32[24,1024]{1,0:T(8,128)} %copy-done.3, f32[24,1024]{1,0:T(8,128)} %copy-done.10, f32[24,1024]{1,0:T(8,128)} %copy-done.11, f32[24,1024]{1,0:T(8,128)} %copy-done.13, f32[4,24,128]{2,1,0:T(8,128)} %reshape.78.start_ref.refs_4_, f32[64,80,128]{2,1,0:T(8,128)} %copy-done, ...), custom_call_target="tpu_custom_call" | custom-call | flops 40000000 | bytes 1500000 | tf_op jit(solution)/shard_map/step3/pallas_call | solution.py:371
  185.1 2.6 collective-permute-done.14.c_ref
  187.7 3.0 %collective-permute-done.13.b_ref = f32[24,1024]{1,0:T(8,128)S(1)} collective-permute-done((f32[24,1024]{1,0:T(8,128)S(1)}, f32[24,1024]{1,0:T(8,128)S(1)}, u32[]{:S(2)}, u32[]{:S(2)}) %collective-permute-start.13) | collective-permute-done | bytes 98336 | tf_op jit(solution)/shard_map/ppermute | solution.py:268
  193.7 3.8 %spectrum.1 = (f32[1024,128]{1,0:T(8,128)}, f32[512,128]{1,0:T(8,128)}) custom-call(s32[1]{0:T(128)} %bitcast.index_ref, f32[1024,32]{1,0:T(8,128)} %copy.40.spectrum_ref, f32[8,1024]{1,0:T(8,128)} %concatenate.19.extra_ref), custom_call_target="tpu_custom_call" | custom-call | flops 300000000 | bytes 1500000 | tf_op jit(solution)/shard_map/spectrum/pallas_call | solution.py:340
  197.5 3.2 %pencil1.1.pencil_ref = f32[1024,128]{1,0:T(8,128)} custom-call(f32[64,80,128]{2,1,0:T(8,128)} %copy-done, s32[1,4096]{1,0:T(1,128)} %bitcast.48, f32[16,4096]{1,0:T(8,128)} %fusion.3.wave_ref, f32[2,4096]{1,0:T(2,128)} %add_convert_fusion.plane_ref, f32[24,1024]{1,0:T(8,128)} %get-tuple-element.10.refs_8_.refs_9_.unknown_ref), custom_call_target="tpu_custom_call" | custom-call | flops 536870912 | bytes 1500000 | tf_op jit(solution)/shard_map/pencil1/pallas_call | solution.py:391
  200.7 2.6 pencil2.1.pencil_ref
  203.4 2.7 pencil3.1.pencil_ref
  206.0 9.6 %filter.1 = f32[64,16,128]{2,1,0:T(8,128)} custom-call(f32[1024,128]{1,0:T(8,128)} %pencil3.1.pencil_ref, s32[1,4096]{1,0:T(1,128)} %bitcast.51, f32[16,4096]{1,0:T(8,128)} %fusion.3.wave_ref, f32[2,4096]{1,0:T(2,128)} %add_convert_fusion.plane_ref, f32[24,1024]{1,0:T(8,128)} %copy-done.1, f32[24,1024]{1,0:T(8,128)} %copy-done.8, f32[24,1024]{1,0:T(8,128)} %copy-done.7, ...), custom_call_target="tpu_custom_call" | custom-call | flops 2147483648 | bytes 11000000 | tf_op jit(solution)/shard_map/filter/pallas_call | solution.py:406
  215.6 28.0 %all_to_all.20.slots_ref = f32[64,16,128]{2,1,0:T(8,128)} all-to-all(f32[64,16,128]{2,1,0:T(8,128)} %filter.1), channel_id=1, replica_groups=mesh['z'=8,'x'=4,'core'=2,'y'=4] {'z','x','core'}, dimensions={0} | all-to-all | bytes 1048576 | tf_op jit(solution)/shard_map/all_to_all | solution.py:419
  243.6 4.2 %close.1 = f32[128,1024]{1,0:T(8,128)} custom-call(f32[64,16,128]{2,1,0:T(8,128)} %all_to_all.20.slots_ref, bf16[1024,1024]{1,0:T(8,128)(2,1)} %constant.132.clone.high_ref, bf16[1024,1024]{1,0:T(8,128)(2,1)} %constant.133.clone.low_ref), custom_call_target="tpu_custom_call" | custom-call | flops 805306368 | bytes 5500000 | tf_op jit(solution)/shard_map/close/pallas_call | solution.py:425
  249.9 5.5 %update.2.base_ref = f32[32,16,128]{2,1,0:T(8,128)} custom-call(s32[1]{0:T(128)} %bitcast.index_ref, f32[32,16,128]{2,1,0:T(8,128)} %base_ref.1, f32[32,16,4096]{2,1,0:T(8,128)} %factor_ref.3, f32[8,32,1024]{2,1,0:T(8,128)} %bitcast.40), custom_call_target="tpu_custom_call" | custom-call | flops 805306368 | bytes 5500000 | tf_op jit(solution)/shard_map/update/pallas_call | solution.py:272
  255.5 5.6 %update.3 = f32[32,16,128]{2,1,0:T(8,128)} custom-call(s32[1]{0:T(128)} %bitcast.index_ref, f32[32,16,128]{2,1,0:T(8,128)} %update.2.base_ref, f32[32,16,4096]{2,1,0:T(8,128)} %factor_ref.3, f32[8,32,1024]{2,1,0:T(8,128)} %bitcast.41), custom_call_target="tpu_custom_call" | custom-call | flops 805306368 | bytes 5500000 | tf_op jit(solution)/shard_map/update/pallas_call | solution.py:272
  (124 shorter events, 56.0 us)
Async XLA Ops:
  8.6 11.0 %all-to-all-start = ((f32[4,1,64]{2,1,0:T(1,128)}), f32[4,1,64]{2,1,0:T(1,128)S(1)}, u32[]{:S(2)}, u32[]{:S(2)}) async-start(f32[4,1,64]{2,1,0:T(1,128)} %broadcast_in_dim.28), calls=%async_computation | async-start | bytes 4096 | tf_op jit(solution)/shard_map/all_to_all | solution.py:317
  13.6 127.2 %all-gather.7.cloned.1.call-start = ((), (), s32[]{:S(2)}) async-start(), calls=%async_computation.4 | async-start | bytes 3538944 | tf_op jit(solution)/shard_map/all_gather | solution.py:303
  20.5 15.7 %all-to-all-start.1 = ((f32[8,1,1536]{2,1,0:T(1,128)}), f32[8,1,1536]{2,1,0:T(1,128)S(1)}, u32[]{:S(2)}, u32[]{:S(2)}) async-start(f32[8,1,1536]{2,1,0:T(1,128)} %reshape.88), calls=%async_computation.1 | async-start | bytes 98304 | tf_op jit(solution)/shard_map/all_to_all | solution.py:328
  36.2 90.1 %all-to-all-start.2 = ((f32[64,80,128]{2,1,0:T(8,128)}), f32[64,80,128]{2,1,0:T(8,128)S(1)}, u32[]{:S(2)}, u32[]{:S(2)}) async-start(f32[64,80,128]{2,1,0:T(8,128)} %pack.1), calls=%async_computation.2 | async-start | bytes 5242880 | tf_op jit(solution)/shard_map/all_to_all | solution.py:314
  47.6 202.3 %all-gather.9.cloned.1.call-start = ((), (), s32[]{:S(2)}) async-start(), calls=%async_computation.5 | async-start | bytes 1179648 | tf_op jit(solution)/shard_map/all_gather | solution.py:401
  129.8 1.7 collective-permute-start
  132.4 5.3 %collective-permute-start.1 = (f32[24,1024]{1,0:T(8,128)S(1)}, f32[24,1024]{1,0:T(8,128)S(1)}, u32[]{:S(2)}, u32[]{:S(2)}) collective-permute-start(f32[24,1024]{1,0:T(8,128)S(1)} %add.100.refs_0_), channel_id=1, source_target_pairs={{0,8},{8,16},{16,24},{24,0},{1,9},{9,17},{17,25},{25,1},{2,10},{10... | collective-permute-start | bytes 294920 | tf_op jit(solution)/shard_map/ppermute | solution.py:268
  133.7 7.1 %collective-permute-start.2 = (f32[24,1024]{1,0:T(8,128)S(1)}, f32[24,1024]{1,0:T(8,128)S(1)}, u32[]{:S(2)}, u32[]{:S(2)}) collective-permute-start(f32[24,1024]{1,0:T(8,128)S(1)} %add.100.refs_0_), channel_id=1, source_target_pairs={{0,16},{8,24},{16,0},{24,8},{1,17},{9,25},{17,1},{25,9},{2,18},{10... | collective-permute-start | bytes 294920 | tf_op jit(solution)/shard_map/ppermute | solution.py:268
  136.1 4.7 %collective-permute-start.3 = (f32[24,1024]{1,0:T(8,128)S(1)}, f32[24,1024]{1,0:T(8,128)S(1)}, u32[]{:S(2)}, u32[]{:S(2)}) collective-permute-start(f32[24,1024]{1,0:T(8,128)S(1)} %add.100.refs_0_), channel_id=1, source_target_pairs={{0,24},{8,0},{16,8},{24,16},{1,25},{9,1},{17,9},{25,17},{2,26},{10... | collective-permute-start | bytes 294920 | tf_op jit(solution)/shard_map/ppermute | solution.py:268
  144.1 2.3 collective-permute-start.4
  147.3 6.1 %collective-permute-start.5 = (f32[24,1024]{1,0:T(8,128)S(1)}, f32[24,1024]{1,0:T(8,128)S(1)}, u32[]{:S(2)}, u32[]{:S(2)}) collective-permute-start(f32[24,1024]{1,0:T(8,128)S(1)} %add.101.refs_0_), channel_id=1, source_target_pairs={{0,8},{8,16},{16,24},{24,0},{1,9},{9,17},{17,25},{25,1},{2,10},{10... | collective-permute-start | bytes 294920 | tf_op jit(solution)/shard_map/ppermute | solution.py:268
  148.5 6.8 %collective-permute-start.6 = (f32[24,1024]{1,0:T(8,128)S(1)}, f32[24,1024]{1,0:T(8,128)S(1)}, u32[]{:S(2)}, u32[]{:S(2)}) collective-permute-start(f32[24,1024]{1,0:T(8,128)S(1)} %add.101.refs_0_), channel_id=1, source_target_pairs={{0,16},{8,24},{16,0},{24,8},{1,17},{9,25},{17,1},{25,9},{2,18},{10... | collective-permute-start | bytes 294920 | tf_op jit(solution)/shard_map/ppermute | solution.py:268
  150.7 4.7 %collective-permute-start.7 = (f32[24,1024]{1,0:T(8,128)S(1)}, f32[24,1024]{1,0:T(8,128)S(1)}, u32[]{:S(2)}, u32[]{:S(2)}) collective-permute-start(f32[24,1024]{1,0:T(8,128)S(1)} %add.101.refs_0_), channel_id=1, source_target_pairs={{0,24},{8,0},{16,8},{24,16},{1,25},{9,1},{17,9},{25,17},{2,26},{10... | collective-permute-start | bytes 294920 | tf_op jit(solution)/shard_map/ppermute | solution.py:268
  151.9 41.2 %collective-permute-start.16 = (f32[2,1024]{1,0:T(2,128)S(1)}, f32[2,1024]{1,0:T(2,128)S(1)}, u32[]{:S(2)}, u32[]{:S(2)}) collective-permute-start(f32[2,1024]{1,0:T(2,128)S(1)} %bitcast.53), channel_id=1, source_target_pairs={{128,0},{129,1},{130,2},{131,3}} | collective-permute-start | bytes 24584 | tf_op jit(solution)/shard_map/ppermute | solution.py:338
  161.0 94.4 %all-gather.11.cloned.1.call-start = ((), (), s32[]{:S(2)}) async-start(), calls=%async_computation.6 | async-start | bytes 1179648 | tf_op jit(solution)/shard_map/all_gather | solution.py:422
  161.7 2.3 collective-permute-start.8
  165.0 5.7 %collective-permute-start.9 = (f32[24,1024]{1,0:T(8,128)S(1)}, f32[24,1024]{1,0:T(8,128)S(1)}, u32[]{:S(2)}, u32[]{:S(2)}) collective-permute-start(f32[24,1024]{1,0:T(8,128)S(1)} %add.102.refs_0_), channel_id=1, source_target_pairs={{0,8},{8,16},{16,24},{24,0},{1,9},{9,17},{17,25},{25,1},{2,10},{10... | collective-permute-start | bytes 294920 | tf_op jit(solution)/shard_map/ppermute | solution.py:268
  165.9 6.8 %collective-permute-start.10 = (f32[24,1024]{1,0:T(8,128)S(1)}, f32[24,1024]{1,0:T(8,128)S(1)}, u32[]{:S(2)}, u32[]{:S(2)}) collective-permute-start(f32[24,1024]{1,0:T(8,128)S(1)} %add.102.refs_0_), channel_id=1, source_target_pairs={{0,16},{8,24},{16,0},{24,8},{1,17},{9,25},{17,1},{25,9},{2,18},{10... | collective-permute-start | bytes 294920 | tf_op jit(solution)/shard_map/ppermute | solution.py:268
  168.1 4.8 %collective-permute-start.11 = (f32[24,1024]{1,0:T(8,128)S(1)}, f32[24,1024]{1,0:T(8,128)S(1)}, u32[]{:S(2)}, u32[]{:S(2)}) collective-permute-start(f32[24,1024]{1,0:T(8,128)S(1)} %add.102.refs_0_), channel_id=1, source_target_pairs={{0,24},{8,0},{16,8},{24,16},{1,25},{9,1},{17,9},{25,17},{2,26},{10... | collective-permute-start | bytes 294920 | tf_op jit(solution)/shard_map/ppermute | solution.py:268
  177.3 2.3 collective-permute-start.12
  180.6 20.1 %copy-start.1 = (f32[24,1024]{1,0:T(8,128)}, f32[24,1024]{1,0:T(8,128)S(1)}, u32[]{:S(2)}) copy-start(f32[24,1024]{1,0:T(8,128)S(1)} %add.103.a_ref) | copy-start | bytes 294916
  180.6 4.5 %collective-permute-start.15 = (f32[24,1024]{1,0:T(8,128)S(1)}, f32[24,1024]{1,0:T(8,128)S(1)}, u32[]{:S(2)}, u32[]{:S(2)}) collective-permute-start(f32[24,1024]{1,0:T(8,128)S(1)} %add.103.a_ref), channel_id=1, source_target_pairs={{0,24},{8,0},{16,8},{24,16},{1,25},{9,1},{17,9},{25,17},{2,26},{10... | collective-permute-start | bytes 294920 | tf_op jit(solution)/shard_map/ppermute | solution.py:268
  182.7 5.1 %collective-permute-start.14 = (f32[24,1024]{1,0:T(8,128)S(1)}, f32[24,1024]{1,0:T(8,128)S(1)}, u32[]{:S(2)}, u32[]{:S(2)}) collective-permute-start(f32[24,1024]{1,0:T(8,128)S(1)} %add.103.a_ref), channel_id=1, source_target_pairs={{0,16},{8,24},{16,0},{24,8},{1,17},{9,25},{17,1},{25,9},{2,18},{10... | collective-permute-start | bytes 294920 | tf_op jit(solution)/shard_map/ppermute | solution.py:268
  183.3 7.5 %collective-permute-start.13 = (f32[24,1024]{1,0:T(8,128)S(1)}, f32[24,1024]{1,0:T(8,128)S(1)}, u32[]{:S(2)}, u32[]{:S(2)}) collective-permute-start(f32[24,1024]{1,0:T(8,128)S(1)} %add.103.a_ref), channel_id=1, source_target_pairs={{0,8},{8,16},{16,24},{24,0},{1,9},{9,17},{17,25},{25,1},{2,10},{10... | collective-permute-start | bytes 294920 | tf_op jit(solution)/shard_map/ppermute | solution.py:268
  (19 other events, 102.4 us)
Sparse Core Ops, SparseCore 0:
  19.6 92.0 all-gather.6
  161.2 33.2 all-gather.8
  196.3 42.5 all-gather.10
